TPU v7x, 128 devices: a whole 4x4x4 slice. The times are simulated.
128 devices in a mesh: sx: 16 (over z, y_hi, core), sy: 8 (over y_lo, x).
Axes of the slice: x: 4, y: 4 (y_hi: 2, y_lo: 2; y = y_hi * 2 + y_lo), z: 4, core: 2. Of those that a mesh axis runs over, the one named last changes fastest.
Arguments:
- coeffs: float32 [2, 8, 8, 16, 8, 32, 128], P(None, None, None, 'sx', 'sy'), may hold values from -0.9 to 0.9
Outputs:
- traces: float32 [2, 8, 8, 512, 1024], P(None, None, None, 'sx', 'sy')
All inputs are finite; a program needn't handle non-finite values.
Results may differ from a plain program's by a relative error of at most 0.0019.
Values sent between devices are 32-bit elements; how exact they have to be, the bound alone decides.
A program may use at most 192 MiB of HBM per device.

v0:
```python
import math

import jax
import jax.numpy as jnp
import numpy as np
from jax import lax
from jax.sharding import PartitionSpec as P

N = 8192
Q = 8


def swapped(block, axis, stride):
    count = lax.axis_size(axis)
    route = []
    for low in range(count):
        high = low | 1 << stride
        if high != low and high < count:
            route += [(low, high), (high, low)]
    return lax.ppermute(block, axis, route)


def node_list():
    return (1.0 - np.cos(np.pi * (2.0 * np.arange(Q) + 1.0) / (2.0 * Q))) / 2.0


def cheb_table(child_half):
    cheb_nodes = node_list()
    targets = (child_half + cheb_nodes) / 2.0
    lagrange = np.ones((Q, Q))
    for column in range(Q):
        for other_node in range(Q):
            if other_node != column:
                lagrange[:, column] = (
                    lagrange[:, column]
                    * (targets - cheb_nodes[other_node])
                    / (cheb_nodes[column] - cheb_nodes[other_node])
                )
    return jnp.asarray(lagrange, jnp.float32)


def positions(box_index, source_count):
    cheb_nodes = jnp.asarray(node_list(), jnp.float32)
    return (box_index.astype(jnp.float32)[None, :] + cheb_nodes[:, None]) * (4.0 * source_count / N)


def centers(box_index, source_count):
    return (box_index.astype(jnp.float32) + 0.5) * (N / source_count) - 0.5 * N


def phase_gap(spot_one, spot_two, child_one, child_two, parent_one, parent_two):
    place_one = spot_one[:, None, None, None, :, None]
    place_two = spot_two[None, :, None, None, None, :]
    wave_one = child_one[None, None, :, None, None, None]
    wave_two = child_two[None, None, None, :, None, None]
    base_one = parent_one[None, None, :, None, None, None]
    base_two = parent_two[None, None, None, :, None, None]
    two_pi = 2.0 * math.pi
    speed_one = (2.0 + jnp.sin(two_pi * place_one) * jnp.sin(two_pi * place_two)) / 16.0
    speed_two = (2.0 + jnp.cos(two_pi * place_one) * jnp.cos(two_pi * place_two)) / 16.0
    square_one = speed_one * speed_one
    square_two = speed_two * speed_two
    child_root = jnp.sqrt(square_one * wave_one * wave_one + square_two * wave_two * wave_two)
    parent_root = jnp.sqrt(square_one * base_one * base_one + square_two * base_two * base_two)
    linear = place_one * (wave_one - base_one) + place_two * (wave_two - base_two)
    return two_pi * (linear + child_root - parent_root)


def rotate(current, phase_arg, sign_value):
    cosine = jnp.cos(phase_arg)
    sine_part = sign_value * jnp.sin(phase_arg)
    real_part = current[0] * cosine - current[1] * sine_part
    imag_part = current[1] * cosine + current[0] * sine_part
    return jnp.stack([real_part, imag_part])


def interpolate(turned, lagrange, axis_dim):
    if axis_dim == 0:
        return jnp.einsum("ij,zjabcde->ziabcde", lagrange, turned, precision=lax.Precision.HIGHEST)
    return jnp.einsum("ij,zajbcde->zaibcde", lagrange, turned, precision=lax.Precision.HIGHEST)


def reverse_bits(number, bit_count):
    result_bits = jnp.zeros((), jnp.int32)
    for position in range(bit_count):
        result_bits = result_bits + (number >> position & 1) * (1 << bit_count - 1 - position)
    return result_bits


def select_table(child_bit):
    return jnp.where(child_bit == 1, cheb_table(1), cheb_table(0))


def child_term(
    state, table_bit, spot_one, spot_two, child_one, child_two, parent_one, parent_two, axis_dim
):
    spread = interpolate(state, select_table(table_bit), axis_dim)
    return rotate(
        spread, phase_gap(spot_one, spot_two, child_one, child_two, parent_one, parent_two), 1.0
    )


def local(coeffs):
    place_x = lax.axis_index("sx")
    place_y = lax.axis_index("sy")
    devices_x = lax.axis_size("sx")
    devices_y = lax.axis_size("sy")
    levels_x = devices_x.bit_length() - 1
    levels_y = devices_y.bit_length() - 1
    boxes_x = coeffs.shape[5]
    boxes_y = coeffs.shape[6]
    share_x = boxes_x // devices_x
    share_y = boxes_y // devices_y
    local_x = jnp.arange(boxes_x, dtype=jnp.int32)
    local_y = jnp.arange(boxes_y, dtype=jnp.int32)
    current = coeffs
    source_two = jnp.reshape(place_y, (1,))
    spot_two = positions(local_y, devices_y)
    centre_two = centers(source_two, devices_y)
    for height in range(levels_x):
        count_x = devices_x >> height
        source_x = place_x >> height
        child_bit = source_x & 1
        target_x = local_x * (1 << height) + reverse_bits(place_x, height)
        source_one = jnp.reshape(source_x, (1,))
        parent_one = centers(source_one >> 1, count_x // 2)
        kept_spot = positions(target_x * 2 + child_bit, count_x // 2)
        own_centre = centers(source_one, count_x)
        kept_term = child_term(
            current,
            child_bit,
            kept_spot,
            spot_two,
            own_centre,
            centre_two,
            parent_one,
            centre_two,
            0,
        )
        sent_spot = positions(target_x * 2 + (1 - child_bit), count_x // 2)
        sent_term = child_term(
            current,
            1 - child_bit,
            sent_spot,
            spot_two,
            own_centre,
            centre_two,
            parent_one,
            centre_two,
            0,
        )
        current = kept_term + swapped(sent_term, "sx", height)
    final_x = local_x * devices_x + reverse_bits(place_x, levels_x)
    spot_one = positions(final_x, 1)
    zero_centre = centers(jnp.zeros((1,), jnp.int32), 1)
    for height in range(levels_y):
        count_y = devices_y >> height
        source_y = place_y >> height
        child_bit = source_y & 1
        target_y = local_y * (1 << height) + reverse_bits(place_y, height)
        source_own = jnp.reshape(source_y, (1,))
        parent_two = centers(source_own >> 1, count_y // 2)
        kept_spot = positions(target_y * 2 + child_bit, count_y // 2)
        own_centre = centers(source_own, count_y)
        kept_term = child_term(
            current,
            child_bit,
            spot_one,
            kept_spot,
            zero_centre,
            own_centre,
            zero_centre,
            parent_two,
            1,
        )
        sent_spot = positions(target_y * 2 + (1 - child_bit), count_y // 2)
        sent_term = child_term(
            current,
            1 - child_bit,
            spot_one,
            sent_spot,
            zero_centre,
            own_centre,
            zero_centre,
            parent_two,
            1,
        )
        current = kept_term + swapped(sent_term, "sy", height)
    grouped = jnp.reshape(current, (2, Q, Q, devices_x, share_x, devices_y, share_y))
    grouped = jnp.transpose(grouped, (0, 1, 2, 3, 5, 4, 6))
    combined = jnp.reshape(grouped, (2, Q, Q, devices_x * devices_y, share_x, share_y))
    received = lax.all_to_all(combined, ("sx", "sy"), split_axis=3, concat_axis=3, tiled=True)
    received = jnp.reshape(received, (2, Q, Q, devices_x, devices_y, share_x, share_y))
    split_bits = jnp.reshape(
        received, (2, Q, Q) + (2,) * levels_x + (2,) * levels_y + (share_x, share_y)
    )
    order_x = [3 + levels_x - 1 - position for position in range(levels_x)]
    order_y = [3 + levels_x + levels_y - 1 - position for position in range(levels_y)]
    tail_axis = 3 + levels_x + levels_y
    permuted = jnp.transpose(
        split_bits, tuple([0, 1, 2, tail_axis] + order_x + [tail_axis + 1] + order_y)
    )
    return jnp.reshape(permuted, (2, Q, Q, boxes_x, boxes_y))


def solution(mesh):
    in_specs = (P(None, None, None, "sx", "sy", None, None),)
    out_specs = P(None, None, None, "sx", "sy")
    return jax.shard_map(local, mesh=mesh, in_specs=in_specs, out_specs=out_specs, check_vma=False)
```

profile of v0, /device:TPU:1, one launch (start us, length us, event | category | flops | bytes accessed | tf_op | source)
XLA Modules:
  0.0 595.8 jit_solution(11682463839826254918)
XLA Ops:
  1.6 3.5 fusion.25
  6.0 5.1 multiply_subtract_fusion.12
  14.2 2.8 fusion.22
  17.1 5.1 multiply_subtract_fusion.13
  22.2 3.5 convolution_bitcast_fusion.4
  25.8 5.1 multiply_subtract_fusion.10
  32.4 3.4 collective-permute-start.1
  35.8 3.5 convolution_bitcast_fusion.5
  39.3 5.1 multiply_subtract_fusion.11
  44.5 37.4 %collective-permute-done.1 = f32[2,8,8,1,1,32,128]{6,1,5,2,0,4,3:T(8,128)} collective-permute-done((f32[2,8,8,1,1,32,128]{6,1,5,2,0,4,3:T(8,128)}, f32[2,8,8,1,1,32,128]{6,1,5,2,0,4,3:T(8,128)}, u32[]{:S(2)}, u32[]{:S(2)}) %collective-permute-start.1) | collective-permute-done | bytes 2097184 | tf_op jit(solution)/shard_map/ppermute | solution.py:20
  81.9 3.5 convolution_bitcast_fusion.2
  85.5 5.1 multiply_subtract_fusion.8
  92.1 1.8 collective-permute-start.2
  93.9 3.5 convolution_bitcast_fusion.3
  97.4 5.1 multiply_subtract_fusion.9
  102.6 36.7 %collective-permute-done.2 = f32[2,8,8,1,1,32,128]{6,1,5,2,0,4,3:T(8,128)} collective-permute-done((f32[2,8,8,1,1,32,128]{6,1,5,2,0,4,3:T(8,128)}, f32[2,8,8,1,1,32,128]{6,1,5,2,0,4,3:T(8,128)}, u32[]{:S(2)}, u32[]{:S(2)}) %collective-permute-start.2) | collective-permute-done | bytes 2097184 | tf_op jit(solution)/shard_map/ppermute | solution.py:20
  139.3 3.5 convolution_bitcast_fusion
  142.9 5.1 multiply_subtract_fusion.6
  149.5 3.2 collective-permute-start.3
  152.6 3.5 convolution_bitcast_fusion.1
  156.2 5.6 multiply_subtract_fusion.7
  161.8 35.4 %collective-permute-done.3 = f32[2,8,8,1,1,32,128]{6,1,5,2,0,4,3:T(8,128)} collective-permute-done((f32[2,8,8,1,1,32,128]{6,1,5,2,0,4,3:T(8,128)}, f32[2,8,8,1,1,32,128]{6,1,5,2,0,4,3:T(8,128)}, u32[]{:S(2)}, u32[]{:S(2)}) %collective-permute-start.3) | collective-permute-done | bytes 2097184 | tf_op jit(solution)/shard_map/ppermute | solution.py:20
  197.2 1.9 fusion.3
  199.1 3.1 fusion.14
  202.1 3.1 fusion.16
  207.6 10.9 %multiply_subtract_fusion.5 = (f32[1,8,8,1,1,32,128]{6,1,5,2,0,4,3:T(8,128)S(1)}, f32[1,8,8,1,1,32,128]{6,1,5,2,0,4,3:T(8,128)}, f32[1,8,8,1,1,32,128]{6,1,5,2,0,4,3:T(8,128)S(1)}, f32[1,8,8,1,1,32,128]{6,1,5,2,0,4,3:T(8,128)S(1)}) fusion(f32[2,8,8,1,1,32,128]{6,1,5,2,0,4,3:T(8,128)S(1)} %bitcast.181, f32[]{:T(128)S(6)} %sub.528, f32[]{:T(128)S(6)} %sub.496, ...), kind=kLoop, calls=%fused_computation.67 | loop fusion | flops 13107200 | bytes 8416264 | tf_op jit(solution)/shard_map/sub | solution.py:72
  221.4 43.8 %collective-permute-done.4 = f32[2,8,8,1,1,32,128]{6,1,5,2,0,4,3:T(8,128)S(1)} collective-permute-done((f32[2,8,8,1,1,32,128]{6,1,5,2,0,4,3:T(8,128)}, f32[2,8,8,1,1,32,128]{6,1,5,2,0,4,3:T(8,128)S(1)}, u32[]{:S(2)}, u32[]{:S(2)}) %collective-permute-start.4) | collective-permute-done | bytes 2097184 | tf_op jit(solution)/shard_map/ppermute | solution.py:20
  266.5 2.1 fusion.4
  268.5 3.1 fusion.10
  271.6 3.1 fusion.12
  277.1 10.9 %multiply_subtract_fusion.3 = (f32[1,8,8,1,1,32,128]{6,1,5,2,0,4,3:T(8,128)S(1)}, f32[1,8,8,1,1,32,128]{6,1,5,2,0,4,3:T(8,128)}, f32[1,8,8,1,1,32,128]{6,1,5,2,0,4,3:T(8,128)S(1)}, f32[1,8,8,1,1,32,128]{6,1,5,2,0,4,3:T(8,128)S(1)}) fusion(f32[2,8,8,1,1,32,128]{6,1,5,2,0,4,3:T(8,128)S(1)} %bitcast.183, f32[]{:T(128)S(6)} %sub.529, f32[]{:T(128)S(6)} %sub.505, ...), kind=kLoop, calls=%fused_computation.61 | loop fusion | flops 13107200 | bytes 8416264 | tf_op jit(solution)/shard_map/sub | solution.py:72
  289.5 3.1 collective-permute-start.5
  292.6 42.9 %collective-permute-done.5 = f32[2,8,8,1,1,32,128]{6,1,5,2,0,4,3:T(8,128)S(1)} collective-permute-done((f32[2,8,8,1,1,32,128]{6,1,5,2,0,4,3:T(8,128)}, f32[2,8,8,1,1,32,128]{6,1,5,2,0,4,3:T(8,128)S(1)}, u32[]{:S(2)}, u32[]{:S(2)}) %collective-permute-start.5) | collective-permute-done | bytes 2097184 | tf_op jit(solution)/shard_map/ppermute | solution.py:20
  336.8 2.1 fusion.5
  338.8 3.1 fusion.6
  341.9 3.1 fusion.8
  347.4 10.2 %multiply_subtract_fusion.1 = (f32[1,8,8,1,1,32,128]{6,1,5,2,0,4,3:T(8,128)S(1)}, f32[1,8,8,1,1,32,128]{6,1,5,2,0,4,3:T(8,128)S(1)}, f32[1,8,8,1,1,32,128]{6,1,5...) fusion(f32[2,8,8,1,1,32,128]{6,1,5,2,0,4,3:T(8,128)S(1)} %bitcast.179, f32[]{:T(128)S(6)} %sub.530, f32[]{:T(128)S(6)} %sub.514, ...), kind=kLoop, calls=%fused_computation.55 | loop fusion | flops 13107200 | bytes 8416264 | tf_op jit(solution)/shard_map/sub | solution.py:72
  359.2 41.6 %collective-permute-done.6 = f32[2,8,8,1,1,32,128]{6,1,5,2,0,4,3:T(8,128)S(1)} collective-permute-done((f32[2,8,8,1,1,32,128]{6,1,5,2,0,4,3:T(8,128)S(1)}, f32[2,8,8,1,1,32,128]{6,1,5,2,0,4,3:T(8,128)S(1)}, u32[]{:S(2)}, u32[]{:S(2)}) %collective-permute-start.6) | collective-permute-done | bytes 2097184 | tf_op jit(solution)/shard_map/ppermute | solution.py:20
  401.1 8.4 %reshape.3264 = f32[2,8,8,16,2,8,16]{6,5,1,4,3,2,0:T(8,128)} reshape(f32[2,8,8,1,1,32,128]{6,1,5,2,0,4,3:T(8,128)S(1)} %maximum_add_fusion.6) | data formatting | bytes 4194304 | tf_op jit(solution)/shard_map/reshape | solution.py:189
  409.5 7.1 %copy.139 = f32[2,8,8,16,2,8,16]{6,5,3,4,2,1,0:T(8,128)S(1)} copy(f32[2,8,8,16,2,8,16]{6,5,1,4,3,2,0:T(8,128)} %reshape.3264) | data formatting | bytes 4194304 | tf_op jit(solution)/shard_map/reshape | solution.py:189
  416.6 18.8 %copy.146 = f32[2,8,8,128,2,16]{5,4,2,1,0,3:T(2,128)} copy(f32[2,8,8,128,2,16]{5,3,4,2,1,0:T(8,128)S(1)} %bitcast.176) | data formatting | bytes 4194304 | tf_op jit(solution)/shard_map/reshape | solution.py:191
  435.4 24.8 %reshape.3334 = f32[128,1,4096]{2,1,0:T(1,128)S(1)} reshape(f32[128,2,8,8,2,16]{5,4,3,2,1,0:T(2,128)} %bitcast.177) | data formatting | bytes 4194304
  460.3 44.2 %all_to_all.5 = f32[128,1,4096]{2,1,0:T(1,128)} all-to-all(f32[128,1,4096]{2,1,0:T(1,128)S(1)} %reshape.3334), channel_id=1, replica_groups=mesh['sx'=16,'sy'=8] {'sx','sy'}, dimensions={0} | all-to-all | bytes 4194304 | tf_op jit(solution)/shard_map/all_to_all | solution.py:192
  505.0 7.3 %reduce = f32[128,4096]{1,0:T(8,128)S(1)} reduce(f32[128,1,4096]{2,1,0:T(1,128)} %all_to_all.5, f32[]{:T(128)} %broadcast.5313), dimensions={1}, to_apply=%all_to_all.3.reduce_sub_computation | reduce | bytes 4194308 | tf_op jit(solution)/shard_map/all_to_all | solution.py:192
  512.3 23.7 %reshape.3335 = f32[128,2,8,8,2,16]{5,4,3,2,1,0:T(2,128)} reshape(f32[128,4096]{1,0:T(8,128)S(1)} %reduce) | data formatting | bytes 4194304
  536.0 12.7 %copy.94 = f32[2,8,8,128,2,16]{5,2,4,3,1,0:T(8,128)} copy(f32[2,8,8,128,2,16]{5,4,2,1,0,3:T(2,128)} %bitcast.178) | data formatting | bytes 4194304 | tf_op jit(solution)/shard_map/all_to_all | solution.py:192
  548.8 30.4 %copy.95 = f32[2,8,8,2,2,2,2,2,16,2,2,2]{2,1,11,10,9,8,7,6,5,4,3,0:T(8,128)} copy(f32[2,8,8,2,2,2,2,2,16,2,2,2]{8,2,3,9,10,11,4,5,6,7,1,0:T(8,128)} %bitcast.175) | data formatting | bytes 4194304 | tf_op jit(solution)/shard_map/transpose | solution.py:200
  579.2 16.4 %copy.96 = f32[2,8,8,32,128]{4,3,2,1,0:T(8,128)} copy(f32[2,8,8,32,128]{2,1,4,3,0:T(8,128)} %bitcast.174) | data formatting | bytes 4194304 | tf_op jit(solution)/shard_map/reshape | solution.py:203
  (44 shorter events, 26.3 us)
Async XLA Ops:
  0.0 1.6 copy-start
  1.6 3.5 copy-start.6
  11.1 3.1 copy-start.4
  11.1 3.1 copy-start.5
  12.6 9.6 %collective-permute-start = (f32[2,8,8,1,1,32,128]{6,1,5,2,0,4,3:T(8,128)}, f32[2,8,8,1,1,32,128]{6,1,5,2,0,4,3:T(8,128)}, u32[]{:S(2)}, u32[]{:S(2)}) collective-permute-start(f32[2,8,8,1,1,32,128]{6,1,5,2,0,4,3:T(8,128)} %pad_maximum_fusion), channel_id=1, source_target_pairs={{0,8},{8,0},{16,24},{24,16},{32,40},{40,32},{48,56},{56,48},{64,72... | collective-permute-start | bytes 6291464 | tf_op jit(solution)/shard_map/ppermute | solution.py:20
  32.4 49.5 %collective-permute-start.1 = (f32[2,8,8,1,1,32,128]{6,1,5,2,0,4,3:T(8,128)}, f32[2,8,8,1,1,32,128]{6,1,5,2,0,4,3:T(8,128)}, u32[]{:S(2)}, u32[]{:S(2)}) collective-permute-start(f32[2,8,8,1,1,32,128]{6,1,5,2,0,4,3:T(8,128)} %pad_maximum_fusion.1), channel_id=1, source_target_pairs={{0,16},{16,0},{8,24},{24,8},{32,48},{48,32},{40,56},{56,40},{64,80... | collective-permute-start | bytes 6291464 | tf_op jit(solution)/shard_map/ppermute | solution.py:20
  92.1 47.2 %collective-permute-start.2 = (f32[2,8,8,1,1,32,128]{6,1,5,2,0,4,3:T(8,128)}, f32[2,8,8,1,1,32,128]{6,1,5,2,0,4,3:T(8,128)}, u32[]{:S(2)}, u32[]{:S(2)}) collective-permute-start(f32[2,8,8,1,1,32,128]{6,1,5,2,0,4,3:T(8,128)} %pad_maximum_fusion.2), channel_id=1, source_target_pairs={{0,32},{32,0},{8,40},{40,8},{16,48},{48,16},{24,56},{56,24},{64,96... | collective-permute-start | bytes 6291464 | tf_op jit(solution)/shard_map/ppermute | solution.py:20
  149.5 47.7 %collective-permute-start.3 = (f32[2,8,8,1,1,32,128]{6,1,5,2,0,4,3:T(8,128)}, f32[2,8,8,1,1,32,128]{6,1,5,2,0,4,3:T(8,128)}, u32[]{:S(2)}, u32[]{:S(2)}) collective-permute-start(f32[2,8,8,1,1,32,128]{6,1,5,2,0,4,3:T(8,128)} %pad_maximum_fusion.3), channel_id=1, source_target_pairs={{0,64},{64,0},{8,72},{72,8},{16,80},{80,16},{24,88},{88,24},{32,96... | collective-permute-start | bytes 6291464 | tf_op jit(solution)/shard_map/ppermute | solution.py:20
  220.0 45.1 %collective-permute-start.4 = (f32[2,8,8,1,1,32,128]{6,1,5,2,0,4,3:T(8,128)}, f32[2,8,8,1,1,32,128]{6,1,5,2,0,4,3:T(8,128)S(1)}, u32[]{:S(2)}, u32[]{:S(2)}) collective-permute-start(f32[2,8,8,1,1,32,128]{6,1,5,2,0,4,3:T(8,128)} %pad_maximum_fusion.4), channel_id=1, source_target_pairs={{0,1},{1,0},{2,3},{3,2},{4,5},{5,4},{6,7},{7,6},{8,9},{9,8},{10,11... | collective-permute-start | bytes 6291464 | tf_op jit(solution)/shard_map/ppermute | solution.py:20
  265.1 1.3 copy-start.3
  289.5 45.9 %collective-permute-start.5 = (f32[2,8,8,1,1,32,128]{6,1,5,2,0,4,3:T(8,128)}, f32[2,8,8,1,1,32,128]{6,1,5,2,0,4,3:T(8,128)S(1)}, u32[]{:S(2)}, u32[]{:S(2)}) collective-permute-start(f32[2,8,8,1,1,32,128]{6,1,5,2,0,4,3:T(8,128)} %pad_maximum_fusion.5), channel_id=1, source_target_pairs={{0,2},{2,0},{1,3},{3,1},{4,6},{6,4},{5,7},{7,5},{8,10},{10,8},{9,1... | collective-permute-start | bytes 6291464 | tf_op jit(solution)/shard_map/ppermute | solution.py:20
  335.4 1.3 copy-start.2
  357.8 43.0 %collective-permute-start.6 = (f32[2,8,8,1,1,32,128]{6,1,5,2,0,4,3:T(8,128)S(1)}, f32[2,8,8,1,1,32,128]{6,1,5,2,0,4,3:T(8,128)S(1)}, u32[]{:S(2)}, u32[]{:S(2)}) collective-permute-start(f32[2,8,8,1,1,32,128]{6,1,5,2,0,4,3:T(8,128)S(1)} %pad_maximum_fusion.6), channel_id=1, source_target_pairs={{0,4},{4,0},{1,5},{5,1},{2,6},{6,2},{3,7},{7,3},{8,12},{12,8},{9,1... | collective-permute-start | bytes 6291464 | tf_op jit(solution)/shard_map/ppermute | solution.py:20
  579.2 16.4 %copy-start.1 = (f32[2,8,8,1,1,32,128]{6,5,4,3,2,1,0:T(8,128)S(1)}, f32[2,8,8,1,1,32,128]{6,5,4,3,2,1,0:T(8,128)}, u32[]{:S(2)}) copy-start(f32[2,8,8,1,1,32,128]{6,5,4,3,2,1,0:T(8,128)} %param.45) | copy-start | bytes 6291460
where the time goes:
time: 603 us; the launch traced here: 596 us
  waiting for transfers between devices  238 us (39%)
  local copies, waits for them, and re-layouts  154 us (26%)
  other arithmetic  97 us (16%)
  matrix products  45.9 us (8%)
  blocking collectives  44.2 us (7%)
  starting transfers between devices  15.8 us (3%)
    ppermute x7, waiting for transfers between devices, swapped(): return lax.ppermute(block, axis, route)  238 us
    sub x11, other arithmetic, rotate(): real_part = current[0] * cosine - current[1] * sine_part  73.6 us
    unnamed x16, local copies, waits for them, and re-layouts  52.5 us
    all_to_all x1, blocking collectives, local(): lax.all_to_all(combined, ('sx', 'sy'), split_axis=3, concat_axis=3, tiled...  44.2 us
    transpose x1, local copies, waits for them, and re-layouts, local(): jnp.transpose(split_bits, tuple([0, 1, 2, tail_axis] + order_x + [tail_ax...  30.4 us
    dot_general x8, matrix products, interpolate(): jnp.einsum('ij,zjabcde->ziabcde', lagrange, turned, precision=lax.Precisi...  27.6 us
    reshape x1, local copies, waits for them, and re-layouts, local(): jnp.reshape(grouped, (2, Q, Q, devices_x * devices_y, share_x, share_y))  18.8 us
    dot_general x6, matrix products, interpolate(): jnp.einsum('ij,zajbcde->zaibcde', lagrange, turned, precision=lax.Precisi...  18.4 us
  transfers between devices with their start and end apart: 7, of which 6 were waited for; matrix products, arithmetic and copies ran while one was open for 6% of the time, Pallas kernels for 0%

commit v1 on v0

v1 whole, which is shorter than its diff:
```python
import functools
import math

import jax
import jax.numpy as jnp
import numpy as np
from jax import lax
from jax.experimental import pallas as pl
from jax.experimental.pallas import tpu as pltpu
from jax.sharding import PartitionSpec as P

N = 8192
Q = 8
DX = 16
DY = 8
LX = 4
LY = 3
ROWS = 8
CHUNKS = 2
LANES = 128
MESH = pl.DeviceIdType.MESH


def node_list():
    return (1.0 - np.cos(np.pi * (2.0 * np.arange(Q) + 1.0) / (2.0 * Q))) / 2.0


def cheb_table(child_half):
    nodes = node_list()
    targets = (child_half + nodes) / 2.0
    table = np.ones((Q, Q))
    for m in range(Q):
        for n in range(Q):
            if n != m:
                table[:, m] = table[:, m] * (targets - nodes[n]) / (nodes[m] - nodes[n])
    return table


def spread_weights(axis):
    eye = np.eye(Q)
    parts = []
    for h in range(2):
        table = cheb_table(h).T
        block = np.kron(table, eye) if axis == 0 else np.kron(eye, table)
        parts.append(np.kron(np.eye(2), block))
    full = np.concatenate(parts, axis=1).astype(np.float32)
    high = full.astype(jnp.bfloat16)
    low = (full - high.astype(np.float32)).astype(jnp.bfloat16)
    return np.concatenate([high, high], axis=0), low


def lane_table():
    z = node_list()
    lane = np.arange(LANES)
    z_one = z[(lane // Q) % Q]
    z_two = z[lane % Q]
    rows = [
        z_one,
        z_two,
        (lane // (Q * Q)).astype(np.float64),
        np.cos(2 * np.pi * z_one),
        np.sin(2 * np.pi * z_one),
        np.cos(2 * np.pi * z_two),
        np.sin(2 * np.pi * z_two),
        np.zeros(LANES),
    ]
    return np.stack(rows).astype(np.float32)


def fit(function, count, odd):
    r = 0.5 * np.cos(np.pi * (np.arange(400) + 0.5) / 800)
    basis = np.stack([r ** (2 * k + (1 if odd else 0)) for k in range(count)], axis=1)
    return [float(c) for c in np.linalg.lstsq(basis, function(r), rcond=None)[0]]


SIN_FIT = fit(lambda r: 2.0 * np.sin(np.pi * r), 5, True)
COS_FIT = fit(lambda r: np.cos(np.pi * r), 5, False)


def horner(coefs, z):
    total = coefs[-1] * z + coefs[-2]
    for c in coefs[-3::-1]:
        total = total * z + c
    return total


def turn(cycles):
    r = cycles - jnp.round(cycles)
    z = r * r
    twice_sine = horner(SIN_FIT, z) * r
    cosine = horner(COS_FIT, z)
    return 1.0 - 0.5 * (twice_sine * twice_sine), twice_sine * cosine


def root(v):
    inverse = lax.rsqrt(v)
    s = v * inverse
    return s + (0.5 * inverse) * (v - s * s), inverse


def with_linear(cosine, sine, lin_cos, lin_sin):
    rc = cosine * lin_cos
    ss = sine * lin_sin
    rs = cosine * lin_sin
    sc = sine * lin_cos
    return rc + ss, sc - rs, rc - ss, sc + rs


def kernel(
    x_hbm,
    lane_ref,
    wx_high,
    wx_low,
    wy_high,
    wy_low,
    out_ref,
    x_ref,
    send_buf,
    recv_buf,
    state_a,
    state_b,
    fin,
    tw_x,
    tw_y0,
    tw_y1,
    tw_y2,
    c2_tab,
    load_sem,
    send_sem,
    recv_sem,
):
    ix = lax.axis_index("sx")
    iy = lax.axis_index("sy")
    slots = DX * DY

    load = pltpu.make_async_copy(x_hbm, x_ref, load_sem)
    load.start()

    barrier = pltpu.get_barrier_semaphore()

    def greet(j, carry):
        other = (lax.rem(ix + j // DY, DX), lax.rem(iy + lax.rem(j, DY), DY))
        pl.semaphore_signal(barrier, inc=1, device_id=other, device_id_type=MESH)
        return carry

    lax.fori_loop(1, slots, greet, 0)
    load.wait()

    def pack(dx):
        for part in range(2):
            halves = [
                x_ref[pl.ds(part * 2048 + 2 * dx + g, Q * Q, stride=32), :] for g in range(2)
            ]
            turned = jnp.concatenate(halves, axis=0).T
            for dy in range(DY):
                for c in range(CHUNKS):
                    low = (dy * CHUNKS + c) * ROWS
                    send_buf[c, dx * DY + dy, part] = turned[low : low + ROWS]

    def send(c, dx, dy):
        pltpu.make_async_remote_copy(
            src_ref=send_buf.at[c, dx * DY + dy],
            dst_ref=recv_buf.at[c, iy * DX + ix],
            send_sem=send_sem.at[c],
            recv_sem=recv_sem.at[c],
            device_id=(dx, dy),
            device_id_type=MESH,
        ).start()

    pack(ix)
    for c in range(CHUNKS):
        recv_buf[c, iy * DX + ix] = send_buf[c, ix * DY + iy]
    pl.semaphore_wait(barrier, slots - 1)
    for jy in range(1, DY):
        send(0, ix, lax.rem(iy + jy, DY))

    def pack_and_send(jx, carry):
        dx = lax.rem(ix + jx, DX)
        pack(dx)
        for jy in range(DY):
            send(0, dx, lax.rem(iy + jy, DY))
        return carry

    lax.fori_loop(1, DX, pack_and_send, 0)

    def send_later(j, carry):
        send(1, lax.rem(ix + j // DY, DX), lax.rem(iy + lax.rem(j, DY), DY))
        return carry

    lax.fori_loop(1, slots, send_later, 0)

    z_one = lane_ref[0:1, :]
    z_two = lane_ref[1:2, :]
    g_bit = lane_ref[2:3, :]
    cos_one, sin_one = lane_ref[3:4, :], lane_ref[4:5, :]
    cos_two, sin_two = lane_ref[5:6, :], lane_ref[6:7, :]
    row = lax.broadcasted_iota(jnp.int32, (ROWS, LANES), 0).astype(jnp.float32)
    base_one = (2 * ix).astype(jnp.float32) + g_bit

    def place_one(level, h):
        box = base_one * float(2 << level) + h.astype(jnp.float32)
        count = DX >> (level + 1)
        return jnp.broadcast_to((box + z_one) * (4.0 * count / N), (ROWS, LANES))

    def place_two(c, level, h):
        box = (row + (iy * (CHUNKS * ROWS) + c * ROWS).astype(jnp.float32)) * float(1 << level) + float(h)
        count = DY >> level
        return (box + z_two) * (4.0 * count / N)

    for level in range(LX):
        count = DX >> level
        width = N // count
        fans = 2 << level

        def x_twiddles(step, carry, level=level, count=count, width=width, fans=fans):
            c = step // fans
            h = lax.rem(step, fans)
            c1, s1 = turn(place_one(level, h))
            c2, s2 = turn(place_two(c, 0, 0))
            speed_one = (2.0 + s1 * s2) * (1.0 / 16.0)
            speed_two = (2.0 + c1 * c2) * (1.0 / 16.0)
            square_one = speed_one * speed_one
            square_two = speed_two * speed_two
            for u2 in range(DY // 2):
                k2 = (u2 + 0.5) * (N / DY) - 0.5 * N
                second = square_two * (k2 * k2)
                parents = {}
                for u1 in range(count // 2):
                    child = (u1 + 0.5) * width - 0.5 * N
                    parent = (u1 // 2 + 0.5) * (2 * width) - 0.5 * N
                    if parent not in parents:
                        parents[parent] = root(square_one * (parent * parent) + second)[0]
                    s_parent = parents[parent]
                    s_child, _ = root(square_one * (child * child) + second)
                    total = s_child + s_parent
                    gap = square_one * (child * child - parent * parent) / total
                    cosine, sine = turn(gap)
                    four = with_linear(cosine, sine, cos_one, sin_one)
                    for k in range(4):
                        tw_x[level, c, u2, u1 * fans + h, k] = four[k]
            return carry

        lax.fori_loop(0, CHUNKS * fans, x_twiddles, 0)

    for c in range(CHUNKS):
        for level in range(LY):
            for h in range(2 << level):
                cosine, _ = turn(place_two(c, level + 1, h))
                c2_tab[c, (2 << level) - 2 + h] = cosine

    tw_y = (tw_y0, tw_y1, tw_y2)

    def y_twiddles(step, carry):
        c = step // DX
        h = lax.rem(step, DX)
        c1, _ = turn(place_one(LX - 1, h))
        for level in range(LY):
            for k in range(2 << level):
                gap = c1 * c2_tab[c, (2 << level) - 2 + k] * float((N // 16 << level) // 16)
                cosine, sine = turn(gap)
                four = with_linear(cosine, sine, cos_two, sin_two)
                for q in range(4):
                    tw_y[level][c, h, k, q] = four[q]
        return carry

    lax.fori_loop(0, CHUNKS * DX, y_twiddles, 0)

    def spread(block, high_ref, low_ref):
        high = block.astype(jnp.bfloat16)
        low = (block - high.astype(jnp.float32)).astype(jnp.bfloat16)
        both = jnp.concatenate([high, low], axis=1)
        main = jnp.dot(both, high_ref[...], preferred_element_type=jnp.float32)
        return main + jnp.dot(high, low_ref[...], preferred_element_type=jnp.float32)

    def levels(c, carry):
        pltpu.make_async_remote_copy(
            src_ref=send_buf.at[c, pl.ds(0, slots - 1)],
            dst_ref=recv_buf.at[c, pl.ds(0, slots - 1)],
            send_sem=send_sem.at[c],
            recv_sem=recv_sem.at[c],
            device_id=(ix, iy),
            device_id_type=MESH,
        ).wait_recv()

        for level in range(LX):
            count = DX >> level
            fans = 1 << level
            source = (None, state_a, state_b, state_a)[level]
            target = (state_a, state_b, state_a, state_b)[level]

            def x_level(b2, carry, level=level, count=count, fans=fans, source=source, target=target):
                if level == 0:
                    block = recv_buf[c, pl.ds(b2 * DX, DX)]
                else:
                    block = source[pl.ds(b2 * DX, DX)]
                wide = spread(block.reshape(DX * 2 * ROWS, LANES), wx_high, wx_low)
                u2 = jnp.minimum(b2, DY - 1 - b2)
                for parent in range(count // 2):
                    for old in range(fans):
                        for h in range(2):
                            fan = 2 * old + h
                            re = im = None
                            for bit in range(2):
                                b1 = 2 * parent + bit
                                u1 = min(b1, count - 1 - b1)
                                low = (b1 * fans + old) * 2 * ROWS
                                a_re = wide[low : low + ROWS, h * LANES : (h + 1) * LANES]
                                a_im = wide[low + ROWS : low + 2 * ROWS, h * LANES : (h + 1) * LANES]
                                t_re = tw_x[level, c, u2, u1 * 2 * fans + fan, 2 * bit]
                                t_im = tw_x[level, c, u2, u1 * 2 * fans + fan, 2 * bit + 1]
                                n_re = a_re * t_re - a_im * t_im
                                n_im = a_re * t_im + a_im * t_re
                                re = n_re if re is None else re + n_re
                                im = n_im if im is None else im + n_im
                            slot = parent * 2 * fans + fan
                            if level == LX - 1:
                                target[slot * DY + b2, 0] = re
                                target[slot * DY + b2, 1] = im
                            else:
                                target[b2 * DX + slot, 0] = re
                                target[b2 * DX + slot, 1] = im
                return carry

            lax.fori_loop(0, DY, x_level, 0)

        for level in range(LY):
            count = DY >> level
            fans = 1 << level
            source = (state_b, state_a, state_b)[level]
            target = (state_a, state_b, None)[level]
            table = tw_y[level]

            def y_level(pair, carry, level=level, count=count, fans=fans, source=source, target=target, table=table):
                block = source[pl.ds(pair * 2 * DY, 2 * DY)]
                wide = spread(block.reshape(2 * DY * 2 * ROWS, LANES), wy_high, wy_low)
                for which in range(2):
                    hx = pair * 2 + which
                    for old in range(fans):
                        for h in range(2):
                            fan = 2 * old + h
                            u_re, u_im, w_re, w_im = (table[c, hx, fan, q] for q in range(4))
                            cut = slice(h * LANES, (h + 1) * LANES)
                            for parent in range(count // 2):
                                low_a = (which * DY + 2 * parent * fans + old) * 2 * ROWS
                                low_b = (which * DY + (2 * parent + 1) * fans + old) * 2 * ROWS
                                a_re = wide[low_a : low_a + ROWS, cut]
                                a_im = wide[low_a + ROWS : low_a + 2 * ROWS, cut]
                                b_re = wide[low_b : low_b + ROWS, cut]
                                b_im = wide[low_b + ROWS : low_b + 2 * ROWS, cut]
                                if level == LY - 1:
                                    re = (a_re * u_re - a_im * u_im) + (b_re * w_re - b_im * w_im)
                                    im = (a_re * u_im + a_im * u_re) + (b_re * w_im + b_im * w_re)
                                elif parent < count // 4:
                                    re = (a_re + b_re) * u_re - (a_im - b_im) * u_im
                                    im = (a_im + b_im) * u_re + (a_re - b_re) * u_im
                                else:
                                    re = (a_re + b_re) * w_re + (a_im - b_im) * w_im
                                    im = (a_im + b_im) * w_re - (a_re - b_re) * w_im
                                if level == LY - 1:
                                    fin[0, hx, pl.ds(c * (ROWS * DY) + fan, ROWS, stride=DY), :] = re
                                    fin[1, hx, pl.ds(c * (ROWS * DY) + fan, ROWS, stride=DY), :] = im
                                else:
                                    slot = hx * DY + parent * 2 * fans + fan
                                    target[slot, 0] = re
                                    target[slot, 1] = im
                return carry

            lax.fori_loop(0, DX // 2, y_level, 0)
        return carry

    lax.fori_loop(0, CHUNKS, levels, 0)

    def unpack(hx, carry):
        for part in range(2):
            turned = fin[part, hx].T
            for g in range(2):
                out_ref[pl.ds(part * 2048 + g * DX + hx, Q * Q, stride=32), :] = turned[
                    g * Q * Q : (g + 1) * Q * Q
                ]
        return carry

    lax.fori_loop(0, DX, unpack, 0)

    for c in range(CHUNKS):
        pltpu.make_async_remote_copy(
            src_ref=send_buf.at[c, pl.ds(0, slots - 1)],
            dst_ref=recv_buf.at[c, pl.ds(0, slots - 1)],
            send_sem=send_sem.at[c],
            recv_sem=recv_sem.at[c],
            device_id=(ix, iy),
            device_id_type=MESH,
        ).wait_send()


def local(coeffs):
    rows = 2 * Q * Q * 32
    flat = jnp.reshape(coeffs, (rows, LANES))
    wx_high, wx_low = spread_weights(0)
    wy_high, wy_low = spread_weights(1)
    vmem = pl.BlockSpec(memory_space=pltpu.VMEM)
    slots = DX * DY
    f32 = jnp.float32
    out = pl.pallas_call(
        kernel,
        out_shape=jax.ShapeDtypeStruct((rows, LANES), f32),
        in_specs=[pl.BlockSpec(memory_space=pl.ANY)] + [vmem] * 5,
        out_specs=vmem,
        scratch_shapes=[
            pltpu.VMEM((rows, LANES), f32),
            pltpu.VMEM((CHUNKS, slots, 2, ROWS, LANES), f32),
            pltpu.VMEM((CHUNKS, slots, 2, ROWS, LANES), f32),
            pltpu.VMEM((slots, 2, ROWS, LANES), f32),
            pltpu.VMEM((slots, 2, ROWS, LANES), f32),
            pltpu.VMEM((2, DX, LANES, LANES), f32),
            pltpu.VMEM((LX, CHUNKS, DY // 2, DX, 4, ROWS, LANES), f32),
            pltpu.VMEM((CHUNKS, DX, 2, 4, ROWS, LANES), f32),
            pltpu.VMEM((CHUNKS, DX, 4, 4, ROWS, LANES), f32),
            pltpu.VMEM((CHUNKS, DX, 8, 4, ROWS, LANES), f32),
            pltpu.VMEM((CHUNKS, 14, ROWS, LANES), f32),
            pltpu.SemaphoreType.DMA,
            pltpu.SemaphoreType.DMA((CHUNKS,)),
            pltpu.SemaphoreType.DMA((CHUNKS,)),
        ],
        compiler_params=pltpu.CompilerParams(
            collective_id=0, has_side_effects=True, vmem_limit_bytes=56 << 20
        ),
        name="butterfly",
    )(
        flat,
        jnp.asarray(lane_table()),
        jnp.asarray(wx_high),
        jnp.asarray(wx_low),
        jnp.asarray(wy_high),
        jnp.asarray(wy_low),
    )
    return jnp.reshape(out, (2, Q, Q, 32, LANES))


def solution(mesh):
    in_specs = (P(None, None, None, "sx", "sy", None, None),)
    out_specs = P(None, None, None, "sx", "sy")
    return jax.shard_map(local, mesh=mesh, in_specs=in_specs, out_specs=out_specs, check_vma=False)
```

time: 603 us -> 73 us (0.12); the launches traced: 596 us -> 72.8 us
  waiting for transfers between devices: 238 us -> 0 us
  local copies, waits for them, and re-layouts: 154 us -> 3.14 us
  other arithmetic: 97 us -> 0 us
  Pallas kernels: 0 us -> 69.7 us
  matrix products: 45.9 us -> 0 us
  blocking collectives: 44.2 us -> 0 us
  starting transfers between devices: 15.8 us -> 0 us
    ppermute x7 -> x0, waiting for transfers between devices: 238 us -> none  [swapped(): return lax.ppermute(block, axis, route)]
    sub x11 -> x0, other arithmetic: 73.6 us -> none  [rotate(): real_part = current[0] * cosine - current[1] * sine_part]
    pallas_call x0 -> x1, Pallas kernels: none -> 69.7 us  [local(): pl.pallas_call(kernel, out_shape=jax.ShapeDtypeStruct((rows, LANES), f32)...]
    reshape x4 -> x0, local copies, waits for them, and re-layouts: 50.8 us -> none  [the longest x1 18.8 us: local(): jnp.reshape(grouped, (2, Q, Q, devices_x * devices_y, share_x, share_y))]
    unnamed x16 -> x1, local copies, waits for them, and re-layouts: 52.5 us -> 3.14 us
    dot_general x14 -> x0, matrix products: 45.9 us -> none  [the longest x8 27.6 us: interpolate(): jnp.einsum('ij,zjabcde->ziabcde', lagrange, turned, precision=lax.Precisi...]
    all_to_all x1 -> x0, blocking collectives: 44.2 us -> none  [local(): lax.all_to_all(combined, ('sx', 'sy'), split_axis=3, concat_axis=3, tiled...]
    transpose x1 -> x0, local copies, waits for them, and re-layouts: 30.4 us -> none  [local(): jnp.transpose(split_bits, tuple([0, 1, 2, tail_axis] + order_x + [tail_ax...]
  transfers between devices with their start and end apart: 7 -> 0, of which waited for: 6 -> 0; matrix products, arithmetic and copies ran while one was open for 6% -> 0% of each run, Pallas kernels for 0% -> 0%
where the time goes in v1:
time: 73 us; the launch traced here: 72.8 us
  Pallas kernels  69.7 us (95%)
  local copies, waits for them, and re-layouts  3.14 us (4%)
    pallas_call x1, Pallas kernels, local(): pl.pallas_call(kernel, out_shape=jax.ShapeDtypeStruct((rows, LANES), f32)...  69.7 us
    unnamed x1, local copies, waits for them, and re-layouts  3.14 us

profile of v1, /device:TPU:1, one launch (start us, length us, event | category | flops | bytes accessed | tf_op | source)
XLA Modules:
  0.0 72.8 jit_solution(15510025247843406582)
XLA Ops:
  0.0 69.7 %butterfly.1 = f32[4096,128]{1,0:T(8,128)} custom-call(f32[4096,128]{1,0:T(8,128)} %bitcast.3, f32[8,128]{1,0:T(8,128)} %constant.10.clone.lane_ref, bf16[256,256]{1,0:T(8,128)(2,1)} %constant.11.clone.wx_high, bf16[128,256]{1,0:T(8,128)(2,1)} %constant.12.clone.wx_low, bf16[256,256]{1,0:T(8,128)(2,1)} %constant.13.clone.wy_high, ...), custom_call_target="tpu_custom_call" | custom-call | tf_op jit(solution)/shard_map/butterfly/pallas_call | solution.py:403
  69.7 3.1 %copy.8 = f32[2,8,8,32,128]{4,3,2,1,0:T(8,128)} copy(f32[2,8,8,32,128]{4,3,2,1,0:T(8,128)} %bitcast.2) | data formatting | bytes 4194304

commit v2 on v1

--- a/solution.py
+++ b/solution.py
@@ -36,35 +36,37 @@
     return table
 
 
-def spread_weights(axis):
-    eye = np.eye(Q)
-    parts = []
-    for h in range(2):
-        table = cheb_table(h).T
-        block = np.kron(table, eye) if axis == 0 else np.kron(eye, table)
-        parts.append(np.kron(np.eye(2), block))
-    full = np.concatenate(parts, axis=1).astype(np.float32)
-    high = full.astype(jnp.bfloat16)
-    low = (full - high.astype(np.float32)).astype(jnp.bfloat16)
-    return np.concatenate([high, high], axis=0), low
-
-
-def lane_table():
-    z = node_list()
-    lane = np.arange(LANES)
-    z_one = z[(lane // Q) % Q]
-    z_two = z[lane % Q]
-    rows = [
-        z_one,
-        z_two,
-        (lane // (Q * Q)).astype(np.float64),
-        np.cos(2 * np.pi * z_one),
-        np.sin(2 * np.pi * z_one),
-        np.cos(2 * np.pi * z_two),
-        np.sin(2 * np.pi * z_two),
-        np.zeros(LANES),
-    ]
-    return np.stack(rows).astype(np.float32)
+def pick(index, values):
+    total = jnp.full(index.shape, float(values[0]), jnp.float32)
+    for k in range(1, len(values)):
+        total = jnp.where(index == k, float(values[k]), total)
+    return total
+
+
+def fill_weights(axis, high_ref, low_ref):
+    nodes = node_list()
+    scale = [1.0 / np.prod([nodes[m] - nodes[n] for n in range(Q) if n != m]) for m in range(Q)]
+    shape = (LANES, 2 * LANES)
+    source = lax.broadcasted_iota(jnp.int32, (LANES, 1), 0)
+    target = lax.broadcasted_iota(jnp.int32, (1, 2 * LANES), 1)
+    first, second = source // Q % Q, source % Q
+    t_first, t_second = target // Q % Q, target % Q
+    child = (target // LANES).astype(jnp.float32)
+    if axis == 0:
+        own, other, t_own, t_other = first, second, t_first, t_second
+    else:
+        own, other, t_own, t_other = second, first, t_second, t_first
+    place = (child + pick(t_own, nodes)) * 0.5
+    table = jnp.broadcast_to(pick(own, scale), shape)
+    for n in range(Q):
+        table = table * jnp.where(own == n, 1.0, place - float(nodes[n]))
+    group = source // (Q * Q) * Q + other
+    t_group = target % LANES // (Q * Q) * Q + t_other
+    table = jnp.where(group == t_group, table, 0.0)
+    high = table.astype(jnp.bfloat16)
+    high_ref[0:LANES, :] = high
+    high_ref[LANES : 2 * LANES, :] = high
+    low_ref[...] = (table - high.astype(jnp.float32)).astype(jnp.bfloat16)
 
 
 def fit(function, count, odd):
@@ -108,13 +110,12 @@
 
 def kernel(
     x_hbm,
-    lane_ref,
+    out_ref,
+    x_ref,
     wx_high,
     wx_low,
     wy_high,
     wy_low,
-    out_ref,
-    x_ref,
     send_buf,
     recv_buf,
     state_a,
@@ -128,6 +129,7 @@
     load_sem,
     send_sem,
     recv_sem,
+    row_sem,
 ):
     ix = lax.axis_index("sx")
     iy = lax.axis_index("sy")
@@ -138,12 +140,19 @@
 
     barrier = pltpu.get_barrier_semaphore()
 
-    def greet(j, carry):
-        other = (lax.rem(ix + j // DY, DX), lax.rem(iy + lax.rem(j, DY), DY))
-        pl.semaphore_signal(barrier, inc=1, device_id=other, device_id_type=MESH)
-        return carry
-
-    lax.fori_loop(1, slots, greet, 0)
+    def other_x(j):
+        return lax.rem(ix + j, DX)
+
+    def other_y(j):
+        return lax.rem(iy + j, DY)
+
+    def greet(semaphore, device):
+        pl.semaphore_signal(semaphore, inc=1, device_id=device, device_id_type=MESH)
+
+    for j in range(1, DX):
+        greet(barrier, (other_x(j), iy))
+    for j in range(1, DY):
+        greet(barrier, (ix, other_y(j)))
     load.wait()
 
     def pack(dx):
@@ -167,33 +176,50 @@
             device_id_type=MESH,
         ).start()
 
-    pack(ix)
+    def sent(c):
+        return pltpu.make_async_remote_copy(
+            src_ref=send_buf.at[c, pl.ds(0, slots - 1)],
+            dst_ref=recv_buf.at[c, pl.ds(0, slots - 1)],
+            send_sem=send_sem.at[c],
+            recv_sem=recv_sem.at[c],
+            device_id=(ix, iy),
+            device_id_type=MESH,
+        )
+
+    def pack_all(j, carry):
+        pack(j)
+        return carry
+
+    lax.fori_loop(0, DX, pack_all, 0)
     for c in range(CHUNKS):
         recv_buf[c, iy * DX + ix] = send_buf[c, ix * DY + iy]
-    pl.semaphore_wait(barrier, slots - 1)
-    for jy in range(1, DY):
-        send(0, ix, lax.rem(iy + jy, DY))
-
-    def pack_and_send(jx, carry):
-        dx = lax.rem(ix + jx, DX)
-        pack(dx)
-        for jy in range(DY):
-            send(0, dx, lax.rem(iy + jy, DY))
-        return carry
-
-    lax.fori_loop(1, DX, pack_and_send, 0)
-
-    def send_later(j, carry):
-        send(1, lax.rem(ix + j // DY, DX), lax.rem(iy + lax.rem(j, DY), DY))
-        return carry
-
-    lax.fori_loop(1, slots, send_later, 0)
-
-    z_one = lane_ref[0:1, :]
-    z_two = lane_ref[1:2, :]
-    g_bit = lane_ref[2:3, :]
-    cos_one, sin_one = lane_ref[3:4, :], lane_ref[4:5, :]
-    cos_two, sin_two = lane_ref[5:6, :], lane_ref[6:7, :]
+
+    pl.semaphore_wait(barrier, DX + DY - 2)
+    for j in range(1, DY):
+        greet(row_sem, (ix, other_y(j)))
+    for j in range(1, DY):
+        send(0, ix, other_y(j))
+    for j in range(1, DX):
+        send(0, other_x(j), iy)
+    pl.semaphore_wait(row_sem, DY - 1)
+
+    def send_rest(j, carry):
+        for k in range(1, DY):
+            send(0, other_x(j), other_y(k))
+        return carry
+
+    lax.fori_loop(1, DX, send_rest, 0)
+
+    fill_weights(0, wx_high, wx_low)
+    fill_weights(1, wy_high, wy_low)
+    nodes = node_list()
+    angles = 2.0 * np.pi * nodes
+    lane = lax.broadcasted_iota(jnp.int32, (1, LANES), 1)
+    t_one, t_two = lane // Q % Q, lane % Q
+    z_one, z_two = pick(t_one, nodes), pick(t_two, nodes)
+    cos_one, sin_one = pick(t_one, np.cos(angles)), pick(t_one, np.sin(angles))
+    cos_two, sin_two = pick(t_two, np.cos(angles)), pick(t_two, np.sin(angles))
+    g_bit = (lane // (Q * Q)).astype(jnp.float32)
     row = lax.broadcasted_iota(jnp.int32, (ROWS, LANES), 0).astype(jnp.float32)
     base_one = (2 * ix).astype(jnp.float32) + g_bit
 
@@ -265,6 +291,14 @@
 
     lax.fori_loop(0, CHUNKS * DX, y_twiddles, 0)
 
+    sent(0).wait_send()
+
+    def send_second(j, carry):
+        send(1, other_x(j // DY), other_y(lax.rem(j, DY)))
+        return carry
+
+    lax.fori_loop(1, slots, send_second, 0)
+
     def spread(block, high_ref, low_ref):
         high = block.astype(jnp.bfloat16)
         low = (block - high.astype(jnp.float32)).astype(jnp.bfloat16)
@@ -273,14 +307,7 @@
         return main + jnp.dot(high, low_ref[...], preferred_element_type=jnp.float32)
 
     def levels(c, carry):
-        pltpu.make_async_remote_copy(
-            src_ref=send_buf.at[c, pl.ds(0, slots - 1)],
-            dst_ref=recv_buf.at[c, pl.ds(0, slots - 1)],
-            send_sem=send_sem.at[c],
-            recv_sem=recv_sem.at[c],
-            device_id=(ix, iy),
-            device_id_type=MESH,
-        ).wait_recv()
+        sent(c).wait_recv()
 
         for level in range(LX):
             count = DX >> level
@@ -321,7 +348,7 @@
                                 target[b2 * DX + slot, 1] = im
                 return carry
 
-            lax.fori_loop(0, DY, x_level, 0)
+            lax.fori_loop(0, DY, x_level, 0, unroll=True)
 
         for level in range(LY):
             count = DY >> level
@@ -365,7 +392,7 @@
                                     target[slot, 1] = im
                 return carry
 
-            lax.fori_loop(0, DX // 2, y_level, 0)
+            lax.fori_loop(0, DX // 2, y_level, 0, unroll=True)
         return carry
 
     lax.fori_loop(0, CHUNKS, levels, 0)
@@ -381,32 +408,25 @@
 
     lax.fori_loop(0, DX, unpack, 0)
 
-    for c in range(CHUNKS):
-        pltpu.make_async_remote_copy(
-            src_ref=send_buf.at[c, pl.ds(0, slots - 1)],
-            dst_ref=recv_buf.at[c, pl.ds(0, slots - 1)],
-            send_sem=send_sem.at[c],
-            recv_sem=recv_sem.at[c],
-            device_id=(ix, iy),
-            device_id_type=MESH,
-        ).wait_send()
+    sent(1).wait_send()
 
 
 def local(coeffs):
     rows = 2 * Q * Q * 32
     flat = jnp.reshape(coeffs, (rows, LANES))
-    wx_high, wx_low = spread_weights(0)
-    wy_high, wy_low = spread_weights(1)
-    vmem = pl.BlockSpec(memory_space=pltpu.VMEM)
     slots = DX * DY
     f32 = jnp.float32
     out = pl.pallas_call(
         kernel,
         out_shape=jax.ShapeDtypeStruct((rows, LANES), f32),
-        in_specs=[pl.BlockSpec(memory_space=pl.ANY)] + [vmem] * 5,
-        out_specs=vmem,
+        in_specs=[pl.BlockSpec(memory_space=pltpu.HBM)],
+        out_specs=pl.BlockSpec(memory_space=pltpu.VMEM),
         scratch_shapes=[
             pltpu.VMEM((rows, LANES), f32),
+            pltpu.VMEM((2 * LANES, 2 * LANES), jnp.bfloat16),
+            pltpu.VMEM((LANES, 2 * LANES), jnp.bfloat16),
+            pltpu.VMEM((2 * LANES, 2 * LANES), jnp.bfloat16),
+            pltpu.VMEM((LANES, 2 * LANES), jnp.bfloat16),
             pltpu.VMEM((CHUNKS, slots, 2, ROWS, LANES), f32),
             pltpu.VMEM((CHUNKS, slots, 2, ROWS, LANES), f32),
             pltpu.VMEM((slots, 2, ROWS, LANES), f32),
@@ -420,19 +440,13 @@
             pltpu.SemaphoreType.DMA,
             pltpu.SemaphoreType.DMA((CHUNKS,)),
             pltpu.SemaphoreType.DMA((CHUNKS,)),
+            pltpu.SemaphoreType.REGULAR,
         ],
         compiler_params=pltpu.CompilerParams(
-            collective_id=0, has_side_effects=True, vmem_limit_bytes=56 << 20
+            collective_id=0, has_side_effects=True, vmem_limit_bytes=32 << 20
         ),
         name="butterfly",
-    )(
-        flat,
-        jnp.asarray(lane_table()),
-        jnp.asarray(wx_high),
-        jnp.asarray(wx_low),
-        jnp.asarray(wy_high),
-        jnp.asarray(wy_low),
-    )
+    )(flat)
     return jnp.reshape(out, (2, Q, Q, 32, LANES))
 
 

time: 73 us -> 46.9 us (0.64)
  Pallas kernels: 69.7 us -> 43.8 us
    pallas_call x1, Pallas kernels: 69.7 us -> 43.8 us  [local(): pl.pallas_call(kernel, out_shape=jax.ShapeDtypeStruct((rows, LANES), f32)...]
    unnamed x1 -> x3, local copies, waits for them, and re-layouts: 3.14 us -> 2.91 us
where the time goes in v2:
time: 46.9 us; the launch traced here: 46.7 us
  Pallas kernels  43.8 us (93%)
  local copies, waits for them, and re-layouts  2.91 us (6%)
    pallas_call x1, Pallas kernels, local(): pl.pallas_call(kernel, out_shape=jax.ShapeDtypeStruct((rows, LANES), f32)...  43.8 us
    unnamed x3, local copies, waits for them, and re-layouts  2.91 us

profile of v2, /device:TPU:1, one launch (start us, length us, event | category | flops | bytes accessed | tf_op | source)
XLA Modules:
  0.0 46.7 jit_solution(9502173736618745948)
XLA Ops:
  0.0 0.0 copy-start
  0.0 1.6 %copy-done = f32[2,8,8,1,1,32,128]{6,5,4,3,2,1,0:T(8,128)S(1)} copy-done((f32[2,8,8,1,1,32,128]{6,5,4,3,2,1,0:T(8,128)S(1)}, f32[2,8,8,1,1,32,128]{6,5,4,3,2,1,0:T(8,128)}, u32[]{:S(2)}) %copy-start) | copy-done | bytes 2097176
  1.6 43.8 %butterfly.1 = f32[4096,128]{1,0:T(8,128)S(1)} custom-call(f32[4096,128]{1,0:T(8,128)S(1)} %bitcast.3), custom_call_target="tpu_custom_call" | custom-call | tf_op jit(solution)/shard_map/butterfly/pallas_call | solution.py:419
  45.4 1.3 %copy.3 = f32[2,8,8,32,128]{4,3,2,1,0:T(8,128)} copy(f32[2,8,8,32,128]{4,3,2,1,0:T(8,128)S(1)} %bitcast.2) | data formatting | bytes 4194304
Async XLA Ops:
  0.0 1.6 %copy-start = (f32[2,8,8,1,1,32,128]{6,5,4,3,2,1,0:T(8,128)S(1)}, f32[2,8,8,1,1,32,128]{6,5,4,3,2,1,0:T(8,128)}, u32[]{:S(2)}) copy-start(f32[2,8,8,1,1,32,128]{6,5,4,3,2,1,0:T(8,128)} %param.1) | copy-start | bytes 6291460

commit v3 on v2

--- a/solution.py
+++ b/solution.py
@@ -17,6 +17,7 @@
 LY = 3
 ROWS = 8
 CHUNKS = 2
+EARLY = 12
 LANES = 128
 MESH = pl.DeviceIdType.MESH
 
@@ -153,7 +154,6 @@
         greet(barrier, (other_x(j), iy))
     for j in range(1, DY):
         greet(barrier, (ix, other_y(j)))
-    load.wait()
 
     def pack(dx):
         for part in range(2):
@@ -187,27 +187,36 @@
         )
 
     def pack_all(j, carry):
-        pack(j)
-        return carry
-
-    lax.fori_loop(0, DX, pack_all, 0)
+        pack(other_x(j))
+        return carry
+
+    def pack_column(j, carry):
+        pack(other_x(j))
+        send(0, other_x(j), iy)
+        return carry
+
+    def send_column(j, carry):
+        send(0, other_x(j), iy)
+        return carry
+
+    def send_rest(j, carry):
+        for k in range(1, DY):
+            send(0, other_x(j), other_y(k))
+        return carry
+
+    load.wait()
+    lax.fori_loop(0, EARLY, pack_all, 0)
     for c in range(CHUNKS):
         recv_buf[c, iy * DX + ix] = send_buf[c, ix * DY + iy]
-
     pl.semaphore_wait(barrier, DX + DY - 2)
     for j in range(1, DY):
         greet(row_sem, (ix, other_y(j)))
     for j in range(1, DY):
         send(0, ix, other_y(j))
-    for j in range(1, DX):
-        send(0, other_x(j), iy)
+    lax.fori_loop(1, EARLY, send_column, 0)
+    if EARLY < DX:
+        lax.fori_loop(EARLY, DX, pack_column, 0)
     pl.semaphore_wait(row_sem, DY - 1)
-
-    def send_rest(j, carry):
-        for k in range(1, DY):
-            send(0, other_x(j), other_y(k))
-        return carry
-
     lax.fori_loop(1, DX, send_rest, 0)
 
     fill_weights(0, wx_high, wx_low)
@@ -406,14 +415,14 @@
                 ]
         return carry
 
-    lax.fori_loop(0, DX, unpack, 0)
+    lax.fori_loop(0, DX, unpack, 0, unroll=4)
 
     sent(1).wait_send()
 
 
 def local(coeffs):
     rows = 2 * Q * Q * 32
-    flat = jnp.reshape(coeffs, (rows, LANES))
+    flat = pltpu.with_memory_space_constraint(jnp.reshape(coeffs, (rows, LANES)), pltpu.HBM)
     slots = DX * DY
     f32 = jnp.float32
     out = pl.pallas_call(

time: 46.9 us -> 44.2 us (0.942)
  local copies, waits for them, and re-layouts: 2.91 us -> 1.32 us
  Pallas kernels: 43.8 us -> 42.8 us
    unnamed x3 -> x1, local copies, waits for them, and re-layouts: 2.91 us -> 1.32 us
    pallas_call x1, Pallas kernels: 43.8 us -> 42.8 us  [local(): pl.pallas_call(kernel, out_shape=jax.ShapeDtypeStruct((rows, LANES), f32)...]
where the time goes in v3:
time: 44.2 us; the launch traced here: 44.1 us
  Pallas kernels  42.8 us (97%)
  local copies, waits for them, and re-layouts  1.32 us (3%)
    pallas_call x1, Pallas kernels, local(): pl.pallas_call(kernel, out_shape=jax.ShapeDtypeStruct((rows, LANES), f32)...  42.8 us
    unnamed x1, local copies, waits for them, and re-layouts  1.32 us

profile of v3, /device:TPU:1, one launch (start us, length us, event | category | flops | bytes accessed | tf_op | source)
XLA Modules:
  0.0 44.1 jit_solution(12428527251817806488)
XLA Ops:
  0.0 42.8 %butterfly.1 = f32[4096,128]{1,0:T(8,128)S(1)} custom-call(f32[4096,128]{1,0:T(8,128)} %bitcast.3), custom_call_target="tpu_custom_call" | custom-call | tf_op jit(solution)/shard_map/butterfly/pallas_call | solution.py:428
  42.8 1.3 %copy.3 = f32[2,8,8,32,128]{4,3,2,1,0:T(8,128)} copy(f32[2,8,8,32,128]{4,3,2,1,0:T(8,128)S(1)} %bitcast.2) | data formatting | bytes 4194304

commit v4 on v3

--- a/solution.py
+++ b/solution.py
@@ -315,6 +315,15 @@
         main = jnp.dot(both, high_ref[...], preferred_element_type=jnp.float32)
         return main + jnp.dot(high, low_ref[...], preferred_element_type=jnp.float32)
 
+    def unpack(hx, carry):
+        for part in range(2):
+            turned = fin[part, hx].T
+            for g in range(2):
+                out_ref[pl.ds(part * 2048 + g * DX + hx, Q * Q, stride=32), :] = turned[
+                    g * Q * Q : (g + 1) * Q * Q
+                ]
+        return carry
+
     def levels(c, carry):
         sent(c).wait_recv()
 
@@ -330,7 +339,7 @@
                 else:
                     block = source[pl.ds(b2 * DX, DX)]
                 wide = spread(block.reshape(DX * 2 * ROWS, LANES), wx_high, wx_low)
-                u2 = jnp.minimum(b2, DY - 1 - b2)
+                u2 = min(b2, DY - 1 - b2)
                 for parent in range(count // 2):
                     for old in range(fans):
                         for h in range(2):
@@ -357,7 +366,8 @@
                                 target[b2 * DX + slot, 1] = im
                 return carry
 
-            lax.fori_loop(0, DY, x_level, 0, unroll=True)
+            for b2 in range(DY):
+                x_level(b2, 0)
 
         for level in range(LY):
             count = DY >> level
@@ -399,23 +409,16 @@
                                     slot = hx * DY + parent * 2 * fans + fan
                                     target[slot, 0] = re
                                     target[slot, 1] = im
+                    if level == LY - 1 and c == CHUNKS - 1:
+                        unpack(hx, 0)
                 return carry
 
-            lax.fori_loop(0, DX // 2, y_level, 0, unroll=True)
-        return carry
-
-    lax.fori_loop(0, CHUNKS, levels, 0)
-
-    def unpack(hx, carry):
-        for part in range(2):
-            turned = fin[part, hx].T
-            for g in range(2):
-                out_ref[pl.ds(part * 2048 + g * DX + hx, Q * Q, stride=32), :] = turned[
-                    g * Q * Q : (g + 1) * Q * Q
-                ]
-        return carry
-
-    lax.fori_loop(0, DX, unpack, 0, unroll=4)
+            for pair in range(DX // 2):
+                y_level(pair, 0)
+        return carry
+
+    for c in range(CHUNKS):
+        levels(c, 0)
 
     sent(1).wait_send()
 

time: 44.2 us -> 43.8 us (level)
  Pallas kernels: 42.8 us -> 42.3 us
    pallas_call x1, Pallas kernels: 42.8 us -> 42.3 us  [local(): pl.pallas_call(kernel, out_shape=jax.ShapeDtypeStruct((rows, LANES), f32)...]
where the time goes in v4:
time: 43.8 us; the launch traced here: 43.6 us
  Pallas kernels  42.3 us (97%)
  local copies, waits for them, and re-layouts  1.32 us (3%)
    pallas_call x1, Pallas kernels, local(): pl.pallas_call(kernel, out_shape=jax.ShapeDtypeStruct((rows, LANES), f32)...  42.3 us
    unnamed x1, local copies, waits for them, and re-layouts  1.32 us

profile of v4, /device:TPU:1, one launch (start us, length us, event | category | flops | bytes accessed | tf_op | source)
XLA Modules:
  0.0 43.6 jit_solution(6542244210710793941)
XLA Ops:
  0.0 42.3 %butterfly.1 = f32[4096,128]{1,0:T(8,128)S(1)} custom-call(f32[4096,128]{1,0:T(8,128)} %bitcast.3), custom_call_target="tpu_custom_call" | custom-call | tf_op jit(solution)/shard_map/butterfly/pallas_call | solution.py:431
  42.3 1.3 %copy.3 = f32[2,8,8,32,128]{4,3,2,1,0:T(8,128)} copy(f32[2,8,8,32,128]{4,3,2,1,0:T(8,128)S(1)} %bitcast.2) | data formatting | bytes 4194304
